TPU v7x, 256 devices: a whole 4x4x8 slice. The times are simulated.
256 devices in a mesh: dp: 16 (over z, y_lo), feat: 16 (over y_hi, x, core).
Axes of the slice: x: 4, y: 4 (y_hi: 2, y_lo: 2; y = y_hi * 2 + y_lo), z: 8, core: 2. Of those that a mesh axis runs over, the one named last changes fastest.
Arguments:
- first_view: bfloat16 [4096, 16384], P('dp', 'feat')
- second_view: bfloat16 [4096, 16384], P('dp', 'feat')
Outputs:
- first_grad: float32 [4096, 16384], P('dp', 'feat')
- second_grad: float32 [4096, 16384], P('dp', 'feat')
- loss_value: float32 [], replicated
All inputs are finite; a program needn't handle non-finite values.
Results may differ from a plain program's by a relative error of at most 0.0029.
Values may be sent and summed in bfloat16 or wider, within the bound.
No kernel may reach another device: no remote copies, remote signals or barrier semaphores. Data moves between devices by JAX's collectives and lax.ppermute only.
A program may use at most 128 MiB of HBM per device.

v0:
```python
import jax
import jax.numpy as jnp
from jax import lax
from jax.sharding import PartitionSpec as P


def partial_gram(local_rows, gathered):
    return lax.dot_general(
        local_rows, gathered, (((1,), (1,)), ((), ())), preferred_element_type=jnp.float32
    )


def per_device(first_view, second_view):
    row_count, feature_local = first_view.shape
    dp_count = lax.axis_size("dp")
    batch_size = row_count * dp_count
    feature_count = feature_local * lax.axis_size("feat")
    float_a = first_view.astype(jnp.float32)
    float_b = second_view.astype(jnp.float32)
    sums_a, sums_b = lax.psum((jnp.sum(float_a, axis=0), jnp.sum(float_b, axis=0)), "dp")
    cent_a = (float_a - sums_a / batch_size).astype(jnp.bfloat16)
    cent_b = (float_b - sums_b / batch_size).astype(jnp.bfloat16)
    whole_a, whole_b = (
        lax.all_gather(cent_a, "dp", axis=0, tiled=True),
        lax.all_gather(cent_b, "dp", axis=0, tiled=True),
    )
    var_a = jnp.sum(jnp.square(whole_a.astype(jnp.float32)), axis=0) / (batch_size - 1)
    var_b = jnp.sum(jnp.square(whole_b.astype(jnp.float32)), axis=0) / (batch_size - 1)
    part_a = partial_gram(cent_a, whole_a)
    part_b = partial_gram(cent_b, whole_b)
    gram_a, gram_b = lax.psum((part_a, part_b), "feat")
    column_count = batch_size // lax.axis_size("feat")
    begin_at = lax.axis_index("feat") * column_count
    own_a = lax.dynamic_slice_in_dim(gram_a, begin_at, column_count, 1)
    own_b = lax.dynamic_slice_in_dim(gram_b, begin_at, column_count, 1)
    gram_sq = jnp.sum(own_a * own_a) + jnp.sum(own_b * own_b)
    prod_a = jnp.dot(gram_a.astype(jnp.bfloat16), whole_a, preferred_element_type=jnp.float32)
    prod_b = jnp.dot(gram_b.astype(jnp.bfloat16), whole_b, preferred_element_type=jnp.float32)
    differ = float_a - float_b
    var_terms = jnp.sum(var_a * var_a) + jnp.sum(var_b * var_b)
    var_sq = jnp.where(lax.axis_index("dp") == 0, var_terms, jnp.float32(0.0))
    diff_sq = jnp.sum(differ * differ)
    total_gram, total_var, total_diff = lax.psum((gram_sq, var_sq, diff_sq), ("dp", "feat"))
    denominator = (batch_size - 1.0) ** 2
    loss_value = (
        25.0 * total_diff / (batch_size * feature_count)
        + (total_gram / denominator - total_var) / feature_count
    )
    weight = 12.5 * (batch_size - 1.0) / batch_size
    first_grad = prod_a / (batch_size - 1.0) - cent_a.astype(jnp.float32) * var_a + weight * differ
    second_grad = prod_b / (batch_size - 1.0) - cent_b.astype(jnp.float32) * var_b - weight * differ
    return (first_grad, second_grad, loss_value)


def solution(mesh):
    placed = (P("dp", "feat"), P("dp", "feat"))
    return jax.shard_map(
        per_device,
        mesh=mesh,
        in_specs=placed,
        out_specs=(P("dp", "feat"), P("dp", "feat"), P()),
        check_vma=False,
    )
```

profile of v0, /device:TPU:2, one launch (start us, length us, event | category | flops | bytes accessed | tf_op | source)
XLA Modules:
  0.0 696.8 jit_solution(16774039973818233824)
XLA Ops:
  7.2 0.0 all-gather.5.cloned.1.call-start
  7.2 2.1 multiply_reduce_fusion.2
  9.3 38.0 %all-reduce.2 = (f32[1024]{0:T(1024)S(1)}, f32[1024]{0:T(1024)S(1)}) all-reduce(f32[1024]{0:T(1024)S(1)} %get-tuple-element.4, f32[1024]{0:T(1024)S(1)} %get-tuple-element.5), channel_id=1, replica_groups=mesh['dp'=16,'feat'=16] {'dp'}, use_global_device_ids=true, to_apply=%region_1.0 | all-reduce | flops 2048 | bytes 16384 | tf_op jit(solution)/shard_map/psum | solution.py:20
  47.4 1.9 fusion.23
  49.3 0.0 copy-start.1
  49.3 0.0 all-gather.5.cloned.1.call-update
  49.4 0.0 all-gather.3.cloned.1.call-start
  49.4 2.0 fusion.22
  51.4 0.0 all-gather.3.cloned.1.call-update
  51.5 0.0 all-reduce.5.cloned.1.call-start
  51.5 177.8 %all-gather.5.cloned.1.call-done = bf16[4096,1024]{1,0:T(8,128)(2,1)} async-done(((bf16[256,1024]{1,0:T(8,128)(2,1)}), bf16[4096,1024]{1,0:T(8,128)(2,1)}) %all-gather.5.cloned.1.call-update) | async-done | bytes 8388624 | tf_op jit(solution)/shard_map/all_gather | solution.py:25
  229.3 7.9 %fusion.25 = f32[256,4096]{1,0:T(8,128)} fusion(bf16[4096,1024]{1,0:T(8,128)(2,1)} %all-gather.5.cloned.1.call-done, bf16[256,1024]{1,0:T(8,128)(2,1)} %param.3, f32[1024]{0:T(1024)S(1)} %broadcast_multiply_fusion.2), kind=kOutput, calls=%fused_computation.23 | convolution fusion | flops 2148270080 | bytes 13111296 | tf_op jit(solution)/shard_map/dot_general | solution.py:8
  237.2 177.9 %all-gather.3.cloned.1.call-done = bf16[4096,1024]{1,0:T(8,128)(2,1)} async-done(((bf16[256,1024]{1,0:T(8,128)(2,1)}), bf16[4096,1024]{1,0:T(8,128)(2,1)}) %all-gather.3.cloned.1.call-update) | async-done | bytes 8388624 | tf_op jit(solution)/shard_map/all_gather | solution.py:24
  415.1 0.0 copy-done.1
  415.1 7.7 %fusion.27 = f32[256,4096]{1,0:T(8,128)} fusion(bf16[4096,1024]{1,0:T(8,128)(2,1)} %all-gather.3.cloned.1.call-done, bf16[256,1024]{1,0:T(8,128)(2,1)S(1)} %copy-done.1, f32[1024]{0:T(1024)S(1)} %broadcast_multiply_fusion.3), kind=kOutput, calls=%fused_computation.24 | convolution fusion | flops 2148270080 | bytes 13111296 | tf_op jit(solution)/shard_map/dot_general | solution.py:8
  422.8 0.0 all-reduce.5.cloned.1.call-update
  422.9 0.0 copy-start
  422.9 5.1 multiply_reduce_fusion
  428.0 0.6 multiply_reduce_fusion.5
  428.6 5.1 multiply_reduce_fusion.1
  433.7 0.6 multiply_reduce_fusion.6
  435.6 152.2 %all-reduce.5.cloned.1.call-done = (f32[256,4096]{1,0:T(8,128)}, f32[256,4096]{1,0:T(8,128)}) async-done(((f32[256,4096]{1,0:T(8,128)}, f32[256,4096]{1,0:T(8,128)}), (f32[256,4096]{1,0:T(8,128)}, f32[256,4096]{1,0:T(8,128)})) %all-reduce.5.cloned.1.call-update) | async-done | bytes 8388624 | tf_op jit(solution)/shard_map/psum | solution.py:31
  587.9 1.7 multiply_reduce_fusion.3
  590.9 81.1 %all-reduce = (f32[]{:T(128)}, f32[]{:T(128)}, f32[]{:T(128)}) all-reduce(f32[]{:T(128)} %get-tuple-element.3, f32[]{:T(128)S(6)} %add.32, f32[]{:T(128)S(6)} %select_n.9), channel_id=1, replica_groups=mesh['dp'=16,'feat'=16] {'dp','feat'}, use_global_device_ids=true, to_apply=%region_9.0 | all-reduce | flops 3 | bytes 24 | tf_op jit(solution)/shard_map/psum | solution.py:43
  674.0 0.0 copy-done
  674.0 0.0 copy-start.2
  674.0 8.2 %fusion.13 = f32[256,1024]{1,0:T(8,128)} fusion(bf16[4096,1024]{1,0:T(8,128)(2,1)} %all-gather.5.cloned.1.call-done, f32[256,4096]{1,0:T(8,128)} %get-tuple-element.10, bf16[256,1024]{1,0:T(8,128)(2,1)S(1)} %copy-done, bf16[256,1024]{1,0:T(8,128)(2,1)S(1)} %copy-done.1, f32[1024]{0:T(1024)S(1)} %get-tuple-element.14, f32[1024]{0:T(1024)S(1)} %broadcast_multiply_fusion.2), kind=kOutput, calls=%fused_computation.14 | convolution fusion | flops 2151415808 | bytes 14688256 | tf_op jit(solution)/shard_map/dot_general | solution.py:38
  682.2 0.0 copy-done.2
  682.2 6.9 fusion.19
  (2 shorter events, 0.0 us)
Async XLA Ops:
  7.2 222.2 %all-gather.5.cloned.1.call-start = ((), (), s32[]{:S(2)}) async-start(), calls=%async_computation.1 | async-start | bytes 8912896 | tf_op jit(solution)/shard_map/all_gather | solution.py:25
  49.3 365.8 %copy-start.1 = (bf16[256,1024]{1,0:T(8,128)(2,1)S(1)}, bf16[256,1024]{1,0:T(8,128)(2,1)}, u32[]{:S(2)}) copy-start(bf16[256,1024]{1,0:T(8,128)(2,1)} %param.2) | copy-start | bytes 1572868
  49.4 365.7 %all-gather.3.cloned.1.call-start = ((), (), s32[]{:S(2)}) async-start(), calls=%async_computation | async-start | bytes 8912896 | tf_op jit(solution)/shard_map/all_gather | solution.py:24
  51.5 536.4 %all-reduce.5.cloned.1.call-start = ((), (), s32[]{:S(2)}) async-start(), calls=%async_computation.2 | async-start | bytes 16777216 | tf_op jit(solution)/shard_map/psum | solution.py:31
  422.9 251.1 %copy-start = (bf16[256,1024]{1,0:T(8,128)(2,1)S(1)}, bf16[256,1024]{1,0:T(8,128)(2,1)}, u32[]{:S(2)}) copy-start(bf16[256,1024]{1,0:T(8,128)(2,1)} %param.3) | copy-start | bytes 1572868
  674.0 8.2 %copy-start.2 = (f32[256,4096]{1,0:T(8,128)S(1)}, f32[256,4096]{1,0:T(8,128)}, u32[]{:S(2)}) copy-start(f32[256,4096]{1,0:T(8,128)} %get-tuple-element.9) | copy-start | bytes 12582916
Sparse Core Ops, SparseCore 0:
  49.5 179.7 all-gather.4
  231.7 183.3 all-gather.2
  423.0 164.8 all-reduce.4
where the time goes:
time: 700 us; the launch traced here: 697 us
  waiting for transfers between devices  508 us (73%)
  blocking collectives  119 us (17%)
  matrix products  30.8 us (4%)
  between operations  19.5 us (3%)
  other arithmetic  19.2 us (3%)
    all_gather x1, waiting for transfers between devices, per_device(): lax.all_gather(cent_a, 'dp', axis=0, tiled=True)  178 us
    all_gather x1, waiting for transfers between devices, per_device(): lax.all_gather(cent_b, 'dp', axis=0, tiled=True)  178 us
    psum x1, waiting for transfers between devices, per_device(): gram_a, gram_b = lax.psum((part_a, part_b), 'feat')  152 us
    psum x1, blocking collectives, per_device(): lax.psum((gram_sq, var_sq, diff_sq), ('dp', 'feat'))  81.1 us
    psum x1, blocking collectives, per_device(): lax.psum((jnp.sum(float_a, axis=0), jnp.sum(float_b, axis=0)), 'dp')  38 us
    dot_general x2, matrix products, partial_gram(): lax.dot_general(local_rows, gathered, (((1,), (1,)), ((), ())), preferred...  15.6 us
  transfers between devices with their start and end apart: 3, of which 3 were waited for; matrix products, arithmetic and copies ran while one was open for 3% of the time, Pallas kernels for 0%

commit v1 on v0

v1 whole, which is shorter than its diff:
```python
import jax
import jax.numpy as jnp
from jax import lax
from jax.sharding import Mesh, PartitionSpec as P

AXES = ("z", "yl", "yh", "x", "core")
SIZES = (8, 2, 2, 4, 2)
F32, BF16 = jnp.float32, jnp.bfloat16


def shift(value, axis, step):
    size = lax.axis_size(axis)
    return lax.ppermute(value, axis, [(i, (i + step) % size) for i in range(size)])


def swap(value, axis, bit):
    size = lax.axis_size(axis)
    return lax.ppermute(value, axis, [(i, i ^ bit) for i in range(size)])


def dot_t(left, right):
    return lax.dot_general(left, right, (((1,), (1,)), ((), ())), preferred_element_type=F32)


def reduce_gram(part):
    rows, cols = part.shape
    blocks = part.astype(BF16).reshape(8, rows // 8, cols)
    got = lax.all_to_all(blocks, ("yh", "x"), 0, 0, tiled=True)
    total = jnp.sum(got.astype(F32), axis=0)
    square = jnp.sum(total * total)
    out = jnp.broadcast_to(total.astype(BF16)[None], (8, rows // 8, cols))
    whole = lax.all_to_all(out, ("yh", "x"), 0, 0, tiled=True)
    return whole.reshape(rows, cols), square


def per_device(first_view, second_view):
    rows, feats = first_view.shape
    batch = rows * 16
    total_feats = feats * 16
    is_zero = lax.axis_index("core") == 0
    own = jnp.where(is_zero, first_view, second_view)
    give = jnp.where(is_zero, second_view, first_view)
    raw = jnp.concatenate([own, swap(give, "core", 1)], axis=1)

    up1, dn1 = shift(raw, "z", 1), shift(raw, "z", -1)
    other = swap(raw, "yl", 1)

    sums = jnp.sum(raw.astype(F32), axis=0, keepdims=True)
    sums = sums + swap(sums, "yl", 1)
    for bit in (1, 2, 4):
        sums = sums + swap(sums, "z", bit)
    mean = sums / batch

    up2, dn2 = shift(up1, "z", 1), shift(dn1, "z", -1)
    up3, dn3 = shift(up2, "z", 1), shift(dn2, "z", -1)
    half = rows // 2
    far = jnp.concatenate([shift(up3[:half], "z", 1), shift(dn3[half:], "z", -1)], axis=0)

    def center(value):
        return (value.astype(F32) - mean).astype(BF16)

    mine = center(raw)
    left = jnp.concatenate([mine, center(other)], axis=0)
    group_a = jnp.concatenate([mine, center(up1), center(dn1), center(up2), center(dn2)], axis=0)
    group_b = jnp.concatenate([center(up3), center(dn3), center(far)], axis=0)
    gram_a, square_a = reduce_gram(dot_t(left, group_a))
    gram_b, square_b = reduce_gram(dot_t(left, group_b))

    squares = jnp.sum(jnp.square(group_a.astype(F32)), axis=0, keepdims=True) + jnp.sum(
        jnp.square(group_b.astype(F32)), axis=0, keepdims=True
    )
    var = (squares + swap(squares, "yl", 1)) / (batch - 1)

    differ = first_view.astype(F32) - second_view.astype(F32)
    first_dp = (lax.axis_index("z") == 0) & (lax.axis_index("yl") == 0)
    first_feat = first_dp
    var_sq = jnp.where(first_feat, jnp.sum(var * var), F32(0.0))
    loss = (
        25.0 * jnp.sum(differ * differ) / (batch * total_feats)
        + ((square_a + square_b) / (batch - 1.0) ** 2 - var_sq) / total_feats
    )
    loss = jnp.full((1, 128), loss, F32)
    for axis, bit in (("core", 1), ("x", 1), ("x", 2), ("yl", 1), ("z", 1), ("yh", 1), ("z", 2), ("z", 4)):
        loss = loss + swap(loss, axis, bit)

    def product(lo):
        return jnp.dot(gram_a[lo : lo + rows], group_a, preferred_element_type=F32) + jnp.dot(
            gram_b[lo : lo + rows], group_b, preferred_element_type=F32
        )

    away = swap(product(rows).astype(BF16), "yl", 1)
    prod = product(0) + away.astype(F32)
    term = prod / (batch - 1.0) - mine.astype(F32) * var
    got = swap(term[:, feats:], "core", 1)
    weight = 12.5 * (batch - 1.0) / batch
    kept = term[:, :feats]
    first_grad = jnp.where(is_zero, kept, got) + weight * differ
    second_grad = jnp.where(is_zero, got, kept) - weight * differ
    return first_grad, second_grad, loss[0, 0]


def solution(mesh):
    fine = Mesh(mesh.devices.reshape(SIZES), AXES)
    spec = P(("z", "yl"), ("yh", "x", "core"))
    return jax.shard_map(
        per_device,
        mesh=fine,
        in_specs=(spec, spec),
        out_specs=(spec, spec, P()),
        check_vma=False,
    )
```

time: 700 us -> 264 us (0.38)
  waiting for transfers between devices: 508 us -> 148 us
  blocking collectives: 119 us -> 0 us
  starting transfers between devices: 0.12 us -> 63.8 us
  between operations: 19.5 us -> 3.56 us
  matrix products: 30.8 us -> 20.3 us
    all_gather x2 -> x0, waiting for transfers between devices: 356 us -> none  [the longest x1 178 us: per_device(): lax.all_gather(cent_a, 'dp', axis=0, tiled=True)]
    psum x1 -> x0, waiting for transfers between devices: 152 us -> none  [per_device(): gram_a, gram_b = lax.psum((part_a, part_b), 'feat')]
    psum x2 -> x0, blocking collectives: 119 us -> none  [the longest x1 81.1 us: per_device(): lax.psum((gram_sq, var_sq, diff_sq), ('dp', 'feat'))]
    ppermute x0 -> x25, waiting for transfers between devices: none -> 110 us  [the longest x8 62.5 us: shift(): lax.ppermute(value, axis, [(i, (i + step) % size) for i in range(size)])]
    all_to_all x0 -> x4, waiting for transfers between devices: none -> 38.5 us  [the longest x2 20.3 us: reduce_gram(): whole = lax.all_to_all(out, ('yh', 'x'), 0, 0, tiled=True)]
    ppermute x0 -> x25, starting transfers between devices: none -> 38 us  [the longest x17 21.9 us: swap(): return lax.ppermute(value, axis, [(i, i ^ bit) for i in range(size)])]
    all_to_all x0 -> x4, starting transfers between devices: none -> 25.8 us  [the longest x2 14.3 us: reduce_gram(): got = lax.all_to_all(blocks, ('yh', 'x'), 0, 0, tiled=True)]
    dot_general x4 -> x6, matrix products: 30.8 us -> 20.3 us  [the longest x2 9.65 us: dot_t(): lax.dot_general(left, right, (((1,), (1,)), ((), ())), preferred_element_...]
  transfers between devices with their start and end apart: 3 -> 29, of which waited for: 3 -> 24; matrix products, arithmetic and copies ran while one was open for 3% -> 12% of each run, Pallas kernels for 0% -> 0%
where the time goes in v1:
time: 264 us; the launch traced here: 263 us
  waiting for transfers between devices  148 us (56%)
  starting transfers between devices  63.8 us (24%)
  other arithmetic  21.8 us (8%)
  matrix products  20.3 us (8%)
  local copies, waits for them, and re-layouts  5.45 us (2%)
  between operations  3.56 us (1%)
    ppermute x8, waiting for transfers between devices, shift(): lax.ppermute(value, axis, [(i, (i + step) % size) for i in range(size)])  62.5 us
    ppermute x17, waiting for transfers between devices, swap(): return lax.ppermute(value, axis, [(i, i ^ bit) for i in range(size)])  47.4 us
    ppermute x17, starting transfers between devices, swap(): return lax.ppermute(value, axis, [(i, i ^ bit) for i in range(size)])  21.9 us
    all_to_all x2, waiting for transfers between devices, reduce_gram(): whole = lax.all_to_all(out, ('yh', 'x'), 0, 0, tiled=True)  20.3 us
    all_to_all x2, waiting for transfers between devices, reduce_gram(): got = lax.all_to_all(blocks, ('yh', 'x'), 0, 0, tiled=True)  18.2 us
    ppermute x8, starting transfers between devices, shift(): lax.ppermute(value, axis, [(i, (i + step) % size) for i in range(size)])  16.1 us
    all_to_all x2, starting transfers between devices, reduce_gram(): got = lax.all_to_all(blocks, ('yh', 'x'), 0, 0, tiled=True)  14.3 us
    all_to_all x2, starting transfers between devices, reduce_gram(): whole = lax.all_to_all(out, ('yh', 'x'), 0, 0, tiled=True)  11.5 us
  transfers between devices with their start and end apart: 29, of which 24 were waited for; matrix products, arithmetic and copies ran while one was open for 12% of the time, Pallas kernels for 0%

profile of v1, /device:TPU:2, one launch (start us, length us, event | category | flops | bytes accessed | tf_op | source)
XLA Modules:
  0.0 263.2 jit_solution(1405391990067093912)
XLA Ops:
  0.6 1.3 broadcast_select_fusion.1
  2.0 1.9 collective-permute-done
  4.1 1.7 collective-permute-start.1
  5.7 2.1 collective-permute-done.1
  7.8 2.0 collective-permute-start.2
  9.8 1.7 collective-permute-done.2
  11.6 3.4 %collective-permute-start.3 = (f32[1,2048]{1,0:T(1,128)S(1)}, f32[1,2048]{1,0:T(1,128)S(1)}, u32[]{:S(2)}, u32[]{:S(2)}) collective-permute-start(f32[1,2048]{1,0:T(1,128)S(1)} %add.72), channel_id=1, source_target_pairs={{0,64},{32,96},{64,0},{96,32},{128,192},{160,224},{192,128},{224,1... | collective-permute-start | bytes 24584 | tf_op jit(solution)/shard_map/ppermute | solution.py:18
  14.9 1.6 collective-permute-done.3
  16.6 6.9 %collective-permute-start.4 = (f32[1,2048]{1,0:T(1,128)S(1)}, f32[1,2048]{1,0:T(1,128)S(1)}, u32[]{:S(2)}, u32[]{:S(2)}) collective-permute-start(f32[1,2048]{1,0:T(1,128)S(1)} %add.73), channel_id=1, source_target_pairs={{0,128},{32,160},{64,192},{96,224},{128,0},{160,32},{192,64},{224,... | collective-permute-start | bytes 24584 | tf_op jit(solution)/shard_map/ppermute | solution.py:18
  23.5 1.6 collective-permute-done.4
  25.2 1.3 constant_dynamic-update-slice_fusion
  26.5 4.7 %collective-permute-start.7 = (bf16[256,2048]{1,0:T(8,128)(2,1)S(1)}, bf16[256,2048]{1,0:T(8,128)(2,1)S(1)}, u32[]{:S(2)}, u32[]{:S(2)}) collective-permute-start(bf16[256,2048]{1,0:T(8,128)(2,1)S(1)} %get-tuple-element.12), channel_id=1, source_target_pairs={{0,224},{32,0},{64,32},{96,64},{128,96},{160,128},{192,160},{224,1... | collective-permute-start | bytes 3145736 | tf_op jit(solution)/shard_map/ppermute | solution.py:13
  31.2 19.6 %collective-permute-done.7 = bf16[256,2048]{1,0:T(8,128)(2,1)S(1)} collective-permute-done((bf16[256,2048]{1,0:T(8,128)(2,1)S(1)}, bf16[256,2048]{1,0:T(8,128)(2,1)S(1)}, u32[]{:S(2)}, u32[]{:S(2)}) %collective-permute-start.7) | collective-permute-done | bytes 1048608 | tf_op jit(solution)/shard_map/ppermute | solution.py:13
  50.8 3.7 %collective-permute-start.9 = (bf16[256,2048]{1,0:T(8,128)(2,1)S(1)}, bf16[256,2048]{1,0:T(8,128)(2,1)S(1)}, u32[]{:S(2)}, u32[]{:S(2)}) collective-permute-start(bf16[256,2048]{1,0:T(8,128)(2,1)S(1)} %collective-permute-done.7), channel_id=1, source_target_pairs={{0,224},{32,0},{64,32},{96,64},{128,96},{160,128},{192,160},{224,1... | collective-permute-start | bytes 3145736 | tf_op jit(solution)/shard_map/ppermute | solution.py:13
  54.5 19.6 %collective-permute-done.9 = bf16[256,2048]{1,0:T(8,128)(2,1)S(1)} collective-permute-done((bf16[256,2048]{1,0:T(8,128)(2,1)S(1)}, bf16[256,2048]{1,0:T(8,128)(2,1)S(1)}, u32[]{:S(2)}, u32[]{:S(2)}) %collective-permute-start.9) | collective-permute-done | bytes 1048608 | tf_op jit(solution)/shard_map/ppermute | solution.py:13
  74.2 3.7 %collective-permute-start.11 = (bf16[256,2048]{1,0:T(8,128)(2,1)S(1)}, bf16[256,2048]{1,0:T(8,128)(2,1)S(1)}, u32[]{:S(2)}, u32[]{:S(2)}) collective-permute-start(bf16[256,2048]{1,0:T(8,128)(2,1)S(1)} %collective-permute-done.9), channel_id=1, source_target_pairs={{0,224},{32,0},{64,32},{96,64},{128,96},{160,128},{192,160},{224,1... | collective-permute-start | bytes 3145736 | tf_op jit(solution)/shard_map/ppermute | solution.py:13
  77.9 1.6 collective-permute-start.5
  80.7 1.3 fusion.2
  82.0 15.4 %collective-permute-done.11 = bf16[256,2048]{1,0:T(8,128)(2,1)S(1)} collective-permute-done((bf16[256,2048]{1,0:T(8,128)(2,1)S(1)}, bf16[256,2048]{1,0:T(8,128)(2,1)S(1)}, u32[]{:S(2)}, u32[]{:S(2)}) %collective-permute-start.11) | collective-permute-done | bytes 1048608 | tf_op jit(solution)/shard_map/ppermute | solution.py:13
  97.4 3.8 %collective-permute-start.13 = (bf16[128,2048]{1,0:T(8,128)(2,1)S(1)}, bf16[128,2048]{1,0:T(8,128)(2,1)S(1)}, u32[]{:S(2)}, u32[]{:S(2)}) collective-permute-start(bf16[128,2048]{1,0:T(8,128)(2,1)S(1)} %slice.54), channel_id=1, source_target_pairs={{0,224},{32,0},{64,32},{96,64},{128,96},{160,128},{192,160},{224,1... | collective-permute-start | bytes 1572872 | tf_op jit(solution)/shard_map/ppermute | solution.py:13
  102.8 1.3 fusion.4
  104.1 3.8 %collective-permute-done.13 = bf16[128,2048]{1,0:T(8,128)(2,1)S(1)} collective-permute-done((bf16[128,2048]{1,0:T(8,128)(2,1)S(1)}, bf16[128,2048]{1,0:T(8,128)(2,1)S(1)}, u32[]{:S(2)}, u32[]{:S(2)}) %collective-permute-start.13) | collective-permute-done | bytes 524320 | tf_op jit(solution)/shard_map/ppermute | solution.py:13
  107.9 4.0 %collective-permute-done.12 = bf16[128,2048]{1,0:T(8,128)(2,1)S(1)} collective-permute-done((bf16[128,2048]{1,0:T(8,128)(2,1)S(1)}, bf16[128,2048]{1,0:T(8,128)(2,1)S(1)}, u32[]{:S(2)}, u32[]{:S(2)}) %collective-permute-start.12) | collective-permute-done | bytes 524320 | tf_op jit(solution)/shard_map/ppermute | solution.py:13
  113.1 2.8 %convolution_convert_fusion.1 = bf16[512,768]{1,0:T(8,128)(2,1)} fusion(bf16[256,2048]{1,0:T(8,128)(2,1)S(1)} %get-tuple-element.22, bf16[256,2048]{1,0:T(8,128)(2,1)S(1)} %get-tuple-element.6, bf16[256,2048]{1,0:T(8,128)(2,1)S(1)} %get-tuple-element.24, bf16[256,2048]{1,0:T(8,128)(2,1)S(1)} %get-tuple-element.23, bf16[256,2048]{1,0:T(8,128)(2,1)S(1)} %get-tuple-element.21), kind=kOutput, calls=%fused_computation.20 | convolution fusion | flops 1624637440 | bytes 6029312 | tf_op jit(solution)/shard_map/dot_general | solution.py:22
  115.9 7.5 %all-to-all-start.2 = ((bf16[8,64,768]{2,1,0:T(8,128)(2,1)}), bf16[8,64,768]{2,1,0:T(8,128)(2,1)}, u32[]{:S(2)}, u32[]{:S(2)}) async-start(bf16[8,64,768]{2,1,0:T(8,128)(2,1)} %bitcast.20), calls=%async_computation.2 | async-start | bytes 1572864 | tf_op jit(solution)/shard_map/all_to_all | solution.py:28
  123.3 6.8 %convolution_convert_fusion = bf16[512,1280]{1,0:T(8,128)(2,1)} fusion(bf16[1280,2048]{1,0:T(8,128)(2,1)} %fusion.4, bf16[256,2048]{1,0:T(8,128)(2,1)} %copy-done.7, bf16[256,2048]{1,0:T(8,128)(2,1)S(1)} %get-tuple-element.6), kind=kOutput, calls=%fused_computation.3 | convolution fusion | flops 2689204224 | bytes 8650752 | tf_op jit(solution)/shard_map/dot_general | solution.py:22
  130.2 3.9 %all-to-all-done.2 = bf16[8,64,768]{2,1,0:T(8,128)(2,1)} async-done(((bf16[8,64,768]{2,1,0:T(8,128)(2,1)}), bf16[8,64,768]{2,1,0:T(8,128)(2,1)}, u32[]{:S(2)}, u32[]{:S(2)}) %all-to-all-start.2) | async-done | bytes 786464 | tf_op jit(solution)/shard_map/all_to_all | solution.py:28
  134.1 6.8 %all-to-all-start = ((bf16[8,64,1280]{2,1,0:T(8,128)(2,1)}), bf16[8,64,1280]{2,1,0:T(8,128)(2,1)S(1)}, u32[]{:S(2)}, u32[]{:S(2)}) async-start(bf16[8,64,1280]{2,1,0:T(8,128)(2,1)} %bitcast.19), calls=%async_computation | async-start | bytes 2621440 | tf_op jit(solution)/shard_map/all_to_all | solution.py:28
  140.9 1.3 convert_reduce_fusion.2
  142.9 14.3 %all-to-all-done = bf16[8,64,1280]{2,1,0:T(8,128)(2,1)S(1)} async-done(((bf16[8,64,1280]{2,1,0:T(8,128)(2,1)}), bf16[8,64,1280]{2,1,0:T(8,128)(2,1)S(1)}, u32[]{:S(2)}, u32[]{:S(2)}) %all-to-all-start) | async-done | bytes 1310752 | tf_op jit(solution)/shard_map/all_to_all | solution.py:28
  158.1 6.3 %all-to-all-start.3 = ((bf16[8,64,768]{2,1,0:T(8,128)(2,1)}), bf16[8,64,768]{2,1,0:T(8,128)(2,1)}, u32[]{:S(2)}, u32[]{:S(2)}) async-start(bf16[8,64,768]{2,1,0:T(8,128)(2,1)} %broadcast_in_dim.10), calls=%async_computation.3 | async-start | bytes 1572864 | tf_op jit(solution)/shard_map/all_to_all | solution.py:32
  165.3 14.0 %all-to-all-done.3 = bf16[8,64,768]{2,1,0:T(8,128)(2,1)} async-done(((bf16[8,64,768]{2,1,0:T(8,128)(2,1)}), bf16[8,64,768]{2,1,0:T(8,128)(2,1)}, u32[]{:S(2)}, u32[]{:S(2)}) %all-to-all-start.3) | async-done | bytes 786464 | tf_op jit(solution)/shard_map/all_to_all | solution.py:32
  180.4 5.2 %all-to-all-start.1 = ((bf16[8,64,1280]{2,1,0:T(8,128)(2,1)}), bf16[8,64,1280]{2,1,0:T(8,128)(2,1)S(1)}, u32[]{:S(2)}, u32[]{:S(2)}) async-start(bf16[8,64,1280]{2,1,0:T(8,128)(2,1)} %broadcast_in_dim.9), calls=%async_computation.1 | async-start | bytes 2621440 | tf_op jit(solution)/shard_map/all_to_all | solution.py:32
  185.6 3.7 %multiply_reduce_fusion = f32[2048]{0:T(1024)S(1)} fusion(bf16[1280,2048]{1,0:T(8,128)(2,1)} %fusion.4), kind=kLoop, calls=%fused_computation | loop fusion | flops 7862272 | bytes 5251072 | tf_op jit(solution)/shard_map/reduce_sum | solution.py:69
  190.8 2.1 fusion.12
  192.9 6.3 %all-to-all-done.1 = bf16[8,64,1280]{2,1,0:T(8,128)(2,1)S(1)} async-done(((bf16[8,64,1280]{2,1,0:T(8,128)(2,1)}), bf16[8,64,1280]{2,1,0:T(8,128)(2,1)S(1)}, u32[]{:S(2)}, u32[]{:S(2)}) %all-to-all-start.1) | async-done | bytes 1310752 | tf_op jit(solution)/shard_map/all_to_all | solution.py:32
  199.3 4.2 %fusion.14 = f32[256,2048]{1,0:T(8,128)S(1)} fusion(bf16[256,1280]{1,0:T(8,128)(2,1)S(1)} %bitcast.22, bf16[1280,2048]{1,0:T(8,128)(2,1)} %fusion.4), kind=kOutput, calls=%fused_computation.47 | convolution fusion | flops 1342177280 | bytes 7995392 | tf_op jit(solution)/shard_map/dot_general | solution.py:87
  207.6 4.1 %fusion.13 = f32[256,2048]{1,0:T(8,128)S(1)} fusion(bf16[256,1280]{1,0:T(8,128)(2,1)S(1)} %bitcast.21, bf16[1280,2048]{1,0:T(8,128)(2,1)} %fusion.4), kind=kOutput, calls=%fused_computation.46 | convolution fusion | flops 1342177280 | bytes 7995392 | tf_op jit(solution)/shard_map/dot_general | solution.py:87
  211.7 8.1 %collective-permute-done.14 = bf16[256,2048]{1,0:T(8,128)(2,1)S(1)} collective-permute-done((bf16[256,2048]{1,0:T(8,128)(2,1)S(1)}, bf16[256,2048]{1,0:T(8,128)(2,1)S(1)}, u32[]{:S(2)}, u32[]{:S(2)}) %collective-permute-start.14) | collective-permute-done | bytes 1048608 | tf_op jit(solution)/shard_map/ppermute | solution.py:18
  224.6 3.5 %select_subtract_fusion = (f32[256,1024]{1,0:T(8,128)}, f32[256,1024]{1,0:T(8,128)}, f32[]{:T(128)}) fusion(f32[256,1024]{1,0:T(8,128)} %collective-permute-done.16, f32[256,2048]{1,0:T(8,128)S(1)} %multiply_subtract_fusion, bf16[256,1024]{1,0:T(8,128)(2,1)S(1)} %copy-done.6, bf16[256,1024]{1,0:T(8,128)(2,1)S(1)} %copy-done.5, pred[]{:T(512)S(6)} %eq.9), kind=kLoop, calls=%fused_computation.27 | loop fusion | flops 2621439 | bytes 5242885 | tf_op jit(solution)/shard_map/sub | solution.py:98
  231.0 2.6 collective-permute-done.18
  233.6 2.1 collective-permute-start.19
  235.7 3.0 %collective-permute-done.19 = f32[1,128]{1,0:T(1,128)S(1)} collective-permute-done((f32[1,128]{1,0:T(1,128)S(1)}, f32[1,128]{1,0:T(1,128)S(1)}, u32[]{:S(2)}, u32[]{:S(2)}) %collective-permute-start.19) | collective-permute-done | bytes 544 | tf_op jit(solution)/shard_map/ppermute | solution.py:18
  239.3 2.9 %collective-permute-done.20 = f32[1,128]{1,0:T(1,128)S(1)} collective-permute-done((f32[1,128]{1,0:T(1,128)S(1)}, f32[1,128]{1,0:T(1,128)S(1)}, u32[]{:S(2)}, u32[]{:S(2)}) %collective-permute-start.20) | collective-permute-done | bytes 544 | tf_op jit(solution)/shard_map/ppermute | solution.py:18
  242.2 3.5 %collective-permute-done.21 = f32[1,128]{1,0:T(1,128)S(1)} collective-permute-done((f32[1,128]{1,0:T(1,128)S(1)}, f32[1,128]{1,0:T(1,128)S(1)}, u32[]{:S(2)}, u32[]{:S(2)}) %collective-permute-start.21) | collective-permute-done | bytes 544 | tf_op jit(solution)/shard_map/ppermute | solution.py:18
  246.2 4.6 %collective-permute-done.22 = f32[1,128]{1,0:T(1,128)S(1)} collective-permute-done((f32[1,128]{1,0:T(1,128)S(1)}, f32[1,128]{1,0:T(1,128)S(1)}, u32[]{:S(2)}, u32[]{:S(2)}) %collective-permute-start.22) | collective-permute-done | bytes 544 | tf_op jit(solution)/shard_map/ppermute | solution.py:18
  250.8 4.4 %collective-permute-done.23 = f32[1,128]{1,0:T(1,128)S(1)} collective-permute-done((f32[1,128]{1,0:T(1,128)S(1)}, f32[1,128]{1,0:T(1,128)S(1)}, u32[]{:S(2)}, u32[]{:S(2)}) %collective-permute-start.23) | collective-permute-done | bytes 544 | tf_op jit(solution)/shard_map/ppermute | solution.py:18
  255.3 7.3 %collective-permute-done.24 = f32[1,128]{1,0:T(1,128)S(1)} collective-permute-done((f32[1,128]{1,0:T(1,128)S(1)}, f32[1,128]{1,0:T(1,128)S(1)}, u32[]{:S(2)}, u32[]{:S(2)}) %collective-permute-start.24) | collective-permute-done | bytes 544 | tf_op jit(solution)/shard_map/ppermute | solution.py:18
  (74 shorter events, 20.4 us)
Async XLA Ops:
  1.9 2.0 collective-permute-start
  4.1 3.7 %collective-permute-start.1 = (f32[1,2048]{1,0:T(1,128)S(1)}, f32[1,2048]{1,0:T(1,128)S(1)}, u32[]{:S(2)}, u32[]{:S(2)}) collective-permute-start(f32[1,2048]{1,0:T(1,128)S(1)} %bitcast.32), channel_id=1, source_target_pairs={{0,16},{16,0},{1,17},{17,1},{2,18},{18,2},{3,19},{19,3},{4,20},{20... | collective-permute-start | bytes 24584 | tf_op jit(solution)/shard_map/ppermute | solution.py:18
  7.8 3.7 %collective-permute-start.2 = (f32[1,2048]{1,0:T(1,128)S(1)}, f32[1,2048]{1,0:T(1,128)S(1)}, u32[]{:S(2)}, u32[]{:S(2)}) collective-permute-start(f32[1,2048]{1,0:T(1,128)S(1)} %add.71), channel_id=1, source_target_pairs={{0,32},{32,0},{64,96},{96,64},{128,160},{160,128},{192,224},{224,1... | collective-permute-start | bytes 24584 | tf_op jit(solution)/shard_map/ppermute | solution.py:18
  11.6 5.0 %collective-permute-start.3 = (f32[1,2048]{1,0:T(1,128)S(1)}, f32[1,2048]{1,0:T(1,128)S(1)}, u32[]{:S(2)}, u32[]{:S(2)}) collective-permute-start(f32[1,2048]{1,0:T(1,128)S(1)} %add.72), channel_id=1, source_target_pairs={{0,64},{32,96},{64,0},{96,32},{128,192},{160,224},{192,128},{224,1... | collective-permute-start | bytes 24584 | tf_op jit(solution)/shard_map/ppermute | solution.py:18
  16.6 8.6 %collective-permute-start.4 = (f32[1,2048]{1,0:T(1,128)S(1)}, f32[1,2048]{1,0:T(1,128)S(1)}, u32[]{:S(2)}, u32[]{:S(2)}) collective-permute-start(f32[1,2048]{1,0:T(1,128)S(1)} %add.73), channel_id=1, source_target_pairs={{0,128},{32,160},{64,192},{96,224},{128,0},{160,32},{192,64},{224,... | collective-permute-start | bytes 24584 | tf_op jit(solution)/shard_map/ppermute | solution.py:18
  26.5 96.8 %copy-start.3 = (bf16[256,2048]{1,0:T(8,128)(2,1)}, bf16[256,2048]{1,0:T(8,128)(2,1)S(1)}, u32[]{:S(2)}) copy-start(bf16[256,2048]{1,0:T(8,128)(2,1)S(1)} %get-tuple-element.6) | copy-start | bytes 3145732
  26.5 24.3 %collective-permute-start.7 = (bf16[256,2048]{1,0:T(8,128)(2,1)S(1)}, bf16[256,2048]{1,0:T(8,128)(2,1)S(1)}, u32[]{:S(2)}, u32[]{:S(2)}) collective-permute-start(bf16[256,2048]{1,0:T(8,128)(2,1)S(1)} %get-tuple-element.12), channel_id=1, source_target_pairs={{0,224},{32,0},{64,32},{96,64},{128,96},{160,128},{192,160},{224,1... | collective-permute-start | bytes 3145736 | tf_op jit(solution)/shard_map/ppermute | solution.py:13
  31.2 23.3 %collective-permute-start.6 = (bf16[256,2048]{1,0:T(8,128)(2,1)S(1)}, bf16[256,2048]{1,0:T(8,128)(2,1)S(1)}, u32[]{:S(2)}, u32[]{:S(2)}) collective-permute-start(bf16[256,2048]{1,0:T(8,128)(2,1)S(1)} %get-tuple-element.12), channel_id=1, source_target_pairs={{0,32},{32,64},{64,96},{96,128},{128,160},{160,192},{192,224},{224... | collective-permute-start | bytes 3145736 | tf_op jit(solution)/shard_map/ppermute | solution.py:13
  50.8 23.3 %collective-permute-start.9 = (bf16[256,2048]{1,0:T(8,128)(2,1)S(1)}, bf16[256,2048]{1,0:T(8,128)(2,1)S(1)}, u32[]{:S(2)}, u32[]{:S(2)}) collective-permute-start(bf16[256,2048]{1,0:T(8,128)(2,1)S(1)} %collective-permute-done.7), channel_id=1, source_target_pairs={{0,224},{32,0},{64,32},{96,64},{128,96},{160,128},{192,160},{224,1... | collective-permute-start | bytes 3145736 | tf_op jit(solution)/shard_map/ppermute | solution.py:13
  54.5 23.3 %collective-permute-start.8 = (bf16[256,2048]{1,0:T(8,128)(2,1)S(1)}, bf16[256,2048]{1,0:T(8,128)(2,1)S(1)}, u32[]{:S(2)}, u32[]{:S(2)}) collective-permute-start(bf16[256,2048]{1,0:T(8,128)(2,1)S(1)} %collective-permute-done.6), channel_id=1, source_target_pairs={{0,32},{32,64},{64,96},{96,128},{128,160},{160,192},{192,224},{224... | collective-permute-start | bytes 3145736 | tf_op jit(solution)/shard_map/ppermute | solution.py:13
  74.2 23.2 %collective-permute-start.11 = (bf16[256,2048]{1,0:T(8,128)(2,1)S(1)}, bf16[256,2048]{1,0:T(8,128)(2,1)S(1)}, u32[]{:S(2)}, u32[]{:S(2)}) collective-permute-start(bf16[256,2048]{1,0:T(8,128)(2,1)S(1)} %collective-permute-done.9), channel_id=1, source_target_pairs={{0,224},{32,0},{64,32},{96,64},{128,96},{160,128},{192,160},{224,1... | collective-permute-start | bytes 3145736 | tf_op jit(solution)/shard_map/ppermute | solution.py:13
  77.9 23.3 %collective-permute-start.10 = (bf16[256,2048]{1,0:T(8,128)(2,1)S(1)}, bf16[256,2048]{1,0:T(8,128)(2,1)S(1)}, u32[]{:S(2)}, u32[]{:S(2)}) collective-permute-start(bf16[256,2048]{1,0:T(8,128)(2,1)S(1)} %collective-permute-done.8), channel_id=1, source_target_pairs={{0,32},{32,64},{64,96},{96,128},{128,160},{160,192},{192,224},{224... | collective-permute-start | bytes 3145736 | tf_op jit(solution)/shard_map/ppermute | solution.py:13
  77.9 26.2 %collective-permute-start.5 = (bf16[256,2048]{1,0:T(8,128)(2,1)S(1)}, bf16[256,2048]{1,0:T(8,128)(2,1)S(1)}, u32[]{:S(2)}, u32[]{:S(2)}) collective-permute-start(bf16[256,2048]{1,0:T(8,128)(2,1)S(1)} %get-tuple-element.12), channel_id=1, source_target_pairs={{0,16},{16,0},{1,17},{17,1},{2,18},{18,2},{3,19},{19,3},{4,20},{20... | collective-permute-start | bytes 3145736 | tf_op jit(solution)/shard_map/ppermute | solution.py:18
  97.4 10.5 %collective-permute-start.13 = (bf16[128,2048]{1,0:T(8,128)(2,1)S(1)}, bf16[128,2048]{1,0:T(8,128)(2,1)S(1)}, u32[]{:S(2)}, u32[]{:S(2)}) collective-permute-start(bf16[128,2048]{1,0:T(8,128)(2,1)S(1)} %slice.54), channel_id=1, source_target_pairs={{0,224},{32,0},{64,32},{96,64},{128,96},{160,128},{192,160},{224,1... | collective-permute-start | bytes 1572872 | tf_op jit(solution)/shard_map/ppermute | solution.py:13
  101.2 10.7 %collective-permute-start.12 = (bf16[128,2048]{1,0:T(8,128)(2,1)S(1)}, bf16[128,2048]{1,0:T(8,128)(2,1)S(1)}, u32[]{:S(2)}, u32[]{:S(2)}) collective-permute-start(bf16[128,2048]{1,0:T(8,128)(2,1)S(1)} %slice.53), channel_id=1, source_target_pairs={{0,32},{32,64},{64,96},{96,128},{128,160},{160,192},{192,224},{224... | collective-permute-start | bytes 1572872 | tf_op jit(solution)/shard_map/ppermute | solution.py:13
  113.0 2.8 %copy-start = (bf16[256,2048]{1,0:T(8,128)(2,1)}, bf16[256,2048]{1,0:T(8,128)(2,1)S(1)}, u32[]{:S(2)}) copy-start(bf16[256,2048]{1,0:T(8,128)(2,1)S(1)} %get-tuple-element.24) | copy-start | bytes 3145732
  113.0 2.8 %copy-start.7 = (bf16[256,2048]{1,0:T(8,128)(2,1)}, bf16[256,2048]{1,0:T(8,128)(2,1)S(1)}, u32[]{:S(2)}) copy-start(bf16[256,2048]{1,0:T(8,128)(2,1)S(1)} %get-tuple-element.22) | copy-start | bytes 3145732
  115.9 18.2 %all-to-all-start.2 = ((bf16[8,64,768]{2,1,0:T(8,128)(2,1)}), bf16[8,64,768]{2,1,0:T(8,128)(2,1)}, u32[]{:S(2)}, u32[]{:S(2)}) async-start(bf16[8,64,768]{2,1,0:T(8,128)(2,1)} %bitcast.20), calls=%async_computation.2 | async-start | bytes 1572864 | tf_op jit(solution)/shard_map/all_to_all | solution.py:28
  134.1 23.1 %all-to-all-start = ((bf16[8,64,1280]{2,1,0:T(8,128)(2,1)}), bf16[8,64,1280]{2,1,0:T(8,128)(2,1)S(1)}, u32[]{:S(2)}, u32[]{:S(2)}) async-start(bf16[8,64,1280]{2,1,0:T(8,128)(2,1)} %bitcast.19), calls=%async_computation | async-start | bytes 2621440 | tf_op jit(solution)/shard_map/all_to_all | solution.py:28
  158.1 21.1 %all-to-all-start.3 = ((bf16[8,64,768]{2,1,0:T(8,128)(2,1)}), bf16[8,64,768]{2,1,0:T(8,128)(2,1)}, u32[]{:S(2)}, u32[]{:S(2)}) async-start(bf16[8,64,768]{2,1,0:T(8,128)(2,1)} %broadcast_in_dim.10), calls=%async_computation.3 | async-start | bytes 1572864 | tf_op jit(solution)/shard_map/all_to_all | solution.py:32
  180.4 18.8 %all-to-all-start.1 = ((bf16[8,64,1280]{2,1,0:T(8,128)(2,1)}), bf16[8,64,1280]{2,1,0:T(8,128)(2,1)S(1)}, u32[]{:S(2)}, u32[]{:S(2)}) async-start(bf16[8,64,1280]{2,1,0:T(8,128)(2,1)} %broadcast_in_dim.9), calls=%async_computation.1 | async-start | bytes 2621440 | tf_op jit(solution)/shard_map/all_to_all | solution.py:32
  185.6 3.7 %copy-start.1 = (bf16[256,2048]{1,0:T(8,128)(2,1)S(1)}, bf16[256,2048]{1,0:T(8,128)(2,1)}, u32[]{:S(2)}) copy-start(bf16[256,2048]{1,0:T(8,128)(2,1)} %copy-done) | copy-start | bytes 3145732
  190.0 15.7 %collective-permute-start.15 = (f32[1,2048]{1,0:T(1,128)S(1)}, f32[1,2048]{1,0:T(1,128)S(1)}, u32[]{:S(2)}, u32[]{:S(2)}) collective-permute-start(f32[1,2048]{1,0:T(1,128)S(1)} %bitcast.34), channel_id=1, source_target_pairs={{0,16},{16,0},{1,17},{17,1},{2,18},{18,2},{3,19},{19,3},{4,20},{20... | collective-permute-start | bytes 24584 | tf_op jit(solution)/shard_map/ppermute | solution.py:18
  199.3 4.2 %copy-start.2 = (bf16[256,2048]{1,0:T(8,128)(2,1)S(1)}, bf16[256,2048]{1,0:T(8,128)(2,1)}, u32[]{:S(2)}) copy-start(bf16[256,2048]{1,0:T(8,128)(2,1)} %copy-done) | copy-start | bytes 3145732
  199.3 4.2 %copy-start.9 = (bf16[4,64,768]{2,1,0:T(8,128)(2,1)S(1)}, bf16[4,64,768]{2,1,0:T(8,128)(2,1)}, u32[]{:S(2)}) copy-start(bf16[4,64,768]{2,1,0:T(8,128)(2,1)} %get-tuple-element.16) | copy-start | bytes 1179652
  203.5 2.9 %copy-start.8 = (bf16[4,64,768]{2,1,0:T(8,128)(2,1)S(1)}, bf16[4,64,768]{2,1,0:T(8,128)(2,1)}, u32[]{:S(2)}) copy-start(bf16[4,64,768]{2,1,0:T(8,128)(2,1)} %get-tuple-element.15) | copy-start | bytes 1179652
  204.7 15.1 %collective-permute-start.14 = (bf16[256,2048]{1,0:T(8,128)(2,1)S(1)}, bf16[256,2048]{1,0:T(8,128)(2,1)S(1)}, u32[]{:S(2)}, u32[]{:S(2)}) collective-permute-start(bf16[256,2048]{1,0:T(8,128)(2,1)S(1)} %add_convert_fusion), channel_id=1, source_target_pairs={{0,16},{16,0},{1,17},{17,1},{2,18},{18,2},{3,19},{19,3},{4,20},{20... | collective-permute-start | bytes 3145736 | tf_op jit(solution)/shard_map/ppermute | solution.py:18
  207.6 12.2 %copy-start.4 = (bf16[256,2048]{1,0:T(8,128)(2,1)S(1)}, bf16[256,2048]{1,0:T(8,128)(2,1)}, u32[]{:S(2)}) copy-start(bf16[256,2048]{1,0:T(8,128)(2,1)} %copy-done.3) | copy-start | bytes 3145732
  219.8 4.8 %copy-start.5 = (bf16[256,1024]{1,0:T(8,128)(2,1)S(1)}, bf16[256,1024]{1,0:T(8,128)(2,1)}, u32[]{:S(2)}) copy-start(bf16[256,1024]{1,0:T(8,128)(2,1)} %param.2) | copy-start | bytes 1572868
  219.8 4.8 %copy-start.6 = (bf16[256,1024]{1,0:T(8,128)(2,1)S(1)}, bf16[256,1024]{1,0:T(8,128)(2,1)}, u32[]{:S(2)}) copy-start(bf16[256,1024]{1,0:T(8,128)(2,1)} %param.3) | copy-start | bytes 1572868
  221.6 3.0 %collective-permute-start.16 = (f32[256,1024]{1,0:T(8,128)}, f32[256,1024]{1,0:T(8,128)}, u32[]{:S(2)}, u32[]{:S(2)}) collective-permute-start(f32[256,1024]{1,0:T(8,128)} %slice.59), channel_id=1, source_target_pairs={{0,1},{1,0},{2,3},{3,2},{4,5},{5,4},{6,7},{7,6},{8,9},{9,8},{10,11... | collective-permute-start | bytes 3145736 | tf_op jit(solution)/shard_map/ppermute | solution.py:18
  228.8 1.2 collective-permute-start.17
  230.0 3.5 %collective-permute-start.18 = (f32[1,128]{1,0:T(1,128)S(1)}, f32[1,128]{1,0:T(1,128)S(1)}, u32[]{:S(2)}, u32[]{:S(2)}) collective-permute-start(f32[1,128]{1,0:T(1,128)S(1)} %broadcast_add_fusion), channel_id=1, source_target_pairs={{0,2},{2,0},{4,6},{6,4},{1,3},{3,1},{5,7},{7,5},{8,10},{10,8},{12,... | collective-permute-start | bytes 1544 | tf_op jit(solution)/shard_map/ppermute | solution.py:18
  233.6 5.0 %collective-permute-start.19 = (f32[1,128]{1,0:T(1,128)S(1)}, f32[1,128]{1,0:T(1,128)S(1)}, u32[]{:S(2)}, u32[]{:S(2)}) collective-permute-start(f32[1,128]{1,0:T(1,128)S(1)} %fusion.22), channel_id=1, source_target_pairs={{0,4},{2,6},{4,0},{6,2},{1,5},{3,7},{5,1},{7,3},{8,12},{10,14},{12... | collective-permute-start | bytes 1544 | tf_op jit(solution)/shard_map/ppermute | solution.py:18
  238.6 3.5 %collective-permute-start.20 = (f32[1,128]{1,0:T(1,128)S(1)}, f32[1,128]{1,0:T(1,128)S(1)}, u32[]{:S(2)}, u32[]{:S(2)}) collective-permute-start(f32[1,128]{1,0:T(1,128)S(1)} %add.86), channel_id=1, source_target_pairs={{0,16},{16,0},{1,17},{17,1},{2,18},{18,2},{3,19},{19,3},{4,20},{20... | collective-permute-start | bytes 1544 | tf_op jit(solution)/shard_map/ppermute | solution.py:18
  242.2 3.5 %collective-permute-start.21 = (f32[1,128]{1,0:T(1,128)S(1)}, f32[1,128]{1,0:T(1,128)S(1)}, u32[]{:S(2)}, u32[]{:S(2)}) collective-permute-start(f32[1,128]{1,0:T(1,128)S(1)} %add.87), channel_id=1, source_target_pairs={{0,32},{32,0},{64,96},{96,64},{128,160},{160,128},{192,224},{224,1... | collective-permute-start | bytes 1544 | tf_op jit(solution)/shard_map/ppermute | solution.py:18
  245.7 5.0 %collective-permute-start.22 = (f32[1,128]{1,0:T(1,128)S(1)}, f32[1,128]{1,0:T(1,128)S(1)}, u32[]{:S(2)}, u32[]{:S(2)}) collective-permute-start(f32[1,128]{1,0:T(1,128)S(1)} %add.88), channel_id=1, source_target_pairs={{0,8},{8,0},{1,9},{9,1},{2,10},{10,2},{3,11},{11,3},{4,12},{12,4},... | collective-permute-start | bytes 1544 | tf_op jit(solution)/shard_map/ppermute | solution.py:18
  250.8 4.4 %collective-permute-start.23 = (f32[1,128]{1,0:T(1,128)S(1)}, f32[1,128]{1,0:T(1,128)S(1)}, u32[]{:S(2)}, u32[]{:S(2)}) collective-permute-start(f32[1,128]{1,0:T(1,128)S(1)} %add.89), channel_id=1, source_target_pairs={{0,64},{32,96},{64,0},{96,32},{128,192},{160,224},{192,128},{224,1... | collective-permute-start | bytes 1544 | tf_op jit(solution)/shard_map/ppermute | solution.py:18
  255.2 7.4 %collective-permute-start.24 = (f32[1,128]{1,0:T(1,128)S(1)}, f32[1,128]{1,0:T(1,128)S(1)}, u32[]{:S(2)}, u32[]{:S(2)}) collective-permute-start(f32[1,128]{1,0:T(1,128)S(1)} %add.90), channel_id=1, source_target_pairs={{0,128},{32,160},{64,192},{96,224},{128,0},{160,32},{192,64},{224,... | collective-permute-start | bytes 1544 | tf_op jit(solution)/shard_map/ppermute | solution.py:18
